TPU v7x, 512 devices: a whole 4x4x16 slice. The times are simulated.
512 devices in a mesh: gx: 8 (over y, core), yz: 64 (over x, z).
Axes of the slice: x: 4, y: 4, z: 16, core: 2. Of those that a mesh axis runs over, the one named last changes fastest.
Arguments:
- right_side: float32 [128, 2048, 128], P('gx', 'yz'), may hold values from -6 to 6
- coefficient: float32 [128, 2048, 128], P('gx', 'yz'), may hold values from 0.5 to 8
Outputs:
- solution: float32 [128, 2048, 128], P('gx', 'yz')
All inputs are finite; a program needn't handle non-finite values.
Results may differ from a plain program's by a relative error of at most 0.0001.
Values sent between devices are 32-bit elements; how exact they have to be, the bound alone decides.
A program may use at most 64 MiB of HBM per device.

v0:
```python
import jax
import jax.numpy as jnp
from jax import lax
from jax.sharding import PartitionSpec as P

LEVELS = 4
BITERS = 4
RELAXATION = 0.8


def padded_2(cells, sides, width):
    for axis, dim in sides:
        count = lax.axis_size(axis)
        ends = count - 1
        head = lax.slice_in_dim(cells, 0, width, axis=dim)
        tail = lax.slice_in_dim(cells, cells.shape[dim] - width, cells.shape[dim], axis=dim)
        cells = jnp.concatenate(
            [
                lax.ppermute(tail, axis, [(i, (i + 1) % count) for i in range(ends)]),
                cells,
                lax.ppermute(head, axis, [((i + 1) % count, i) for i in range(ends)]),
            ],
            axis=dim,
        )
    return cells


def neighbours(padded):
    return [
        padded[2:, 1:-1, 1:-1],
        padded[:-2, 1:-1, 1:-1],
        padded[1:-1, 2:, 1:-1],
        padded[1:-1, :-2, 1:-1],
        padded[1:-1, 1:-1, 2:],
        padded[1:-1, 1:-1, :-2],
    ]


def face_weights(padded):
    centre = padded[1:-1, 1:-1, 1:-1]
    return [0.5 * (centre + other) for other in neighbours(padded)]


def diagonal_of(face_list, level_scale):
    summed = face_list[0]
    for weight in face_list[1:]:
        summed = summed + weight
    return level_scale * summed


def operate(padded, face_list, level_scale):
    centre = padded[1:-1, 1:-1, 1:-1]
    others = neighbours(padded)
    summed = face_list[0] * (centre - others[0])
    for position in range(1, 6):
        summed = summed + face_list[position] * (centre - others[position])
    return level_scale * summed


def restrict(values):
    return values.reshape(
        values.shape[0] // 2, 2, values.shape[1] // 2, 2, values.shape[2] // 2, 2
    ).mean(axis=(1, 3, 5))


def prolong(values):
    return jnp.repeat(jnp.repeat(jnp.repeat(values, 2, 0), 2, 1), 2, 2)


def padded_box(values):
    framed = padded_2(values, (("gx", 0), ("yz", 1)), 1)
    return jnp.pad(framed, ((0, 0), (0, 0), (1, 1)))


def padded_slab(values):
    framed = padded_2(values, (("gx", 0),), 1)
    return jnp.pad(framed, ((0, 0), (1, 1), (1, 1)))


def stabilized_solve(source, weight):
    level_scale = 0.25**LEVELS
    face_list = face_weights(padded_slab(weight))

    def apply_op(values):
        return operate(padded_slab(values), face_list, level_scale)

    answer = jnp.zeros_like(source)
    residual = source
    rho_now = lax.psum(jnp.sum(source * residual), "gx")
    rho_prev = rho_now
    direction = residual
    applied = jnp.zeros_like(source)
    step_alpha = jnp.float32(1.0)
    step_omega = jnp.float32(1.0)
    for turn_index in range(BITERS):
        if turn_index > 0:
            beta_factor = rho_now / rho_prev * (step_alpha / step_omega)
            direction = residual + beta_factor * (direction - step_omega * applied)
        applied = apply_op(direction)
        step_alpha = rho_now / lax.psum(jnp.sum(source * applied), "gx")
        middle = residual - step_alpha * applied
        bent_image = apply_op(middle)
        pair_sums = lax.psum((jnp.sum(bent_image * middle), jnp.sum(bent_image * bent_image)), "gx")
        step_omega = pair_sums[0] / pair_sums[1]
        answer = answer + step_alpha * direction + step_omega * middle
        residual = middle - step_omega * bent_image
        if turn_index + 1 < BITERS:
            rho_prev = rho_now
            rho_now = lax.psum(jnp.sum(source * residual), "gx")
    return answer


def per_device(right_side, coefficient):
    source = right_side
    weight = coefficient
    stored = []
    for level_index in range(LEVELS):
        merged = False
        level_scale = 0.25**level_index
        padder = padded_box
        face_list = face_weights(padder(weight))
        diagonal = diagonal_of(face_list, level_scale)
        iterate = RELAXATION * source / diagonal
        iterate = (
            iterate
            + RELAXATION * (source - operate(padder(iterate), face_list, level_scale)) / diagonal
        )
        residual = source - operate(padder(iterate), face_list, level_scale)
        stored.append((source, iterate, face_list, diagonal, merged))
        if level_index == LEVELS - 1:
            residual, weight = (
                lax.all_gather(residual, "yz", axis=1, tiled=True),
                lax.all_gather(weight, "yz", axis=1, tiled=True),
            )
        source = restrict(residual)
        weight = restrict(weight)
    correction = stabilized_solve(source, weight)
    for level_index in reversed(range(LEVELS)):
        source, iterate, face_list, diagonal, merged = stored[level_index]
        level_scale = 0.25**level_index
        padder = padded_box
        widened = prolong(correction)
        if widened.shape[1] != iterate.shape[1]:
            own_rows = iterate.shape[1]
            widened = lax.dynamic_slice_in_dim(
                widened, lax.axis_index("yz") * own_rows, own_rows, 1
            )
        iterate = iterate + widened
        iterate = (
            iterate
            + RELAXATION * (source - operate(padder(iterate), face_list, level_scale)) / diagonal
        )
        correction = iterate
    return correction


def solution(mesh):
    return jax.shard_map(
        per_device,
        mesh=mesh,
        in_specs=(P("gx", "yz", None), P("gx", "yz", None)),
        out_specs=P("gx", "yz", None),
        check_vma=False,
    )
```

profile of v0, /device:TPU:10, one launch (start us, length us, event | category | flops | bytes accessed | tf_op | source)
XLA Modules:
  0.0 719.9 jit_solution(8978130539700495041)
XLA Ops:
  7.7 11.4 %collective-permute-start.2 = (f32[18,1,128]{2,1,0:T(1,128)S(1)}, f32[18,1,128]{2,1,0:T(1,128)S(1)}, u32[]{:S(2)}, u32[]{:S(2)}) collective-permute-start(f32[18,1,128]{2,1,0:T(1,128)S(1)} %get-tuple-element.64), channel_id=1, source_target_pairs={{1,0},{2,1},{3,2},{4,3},{5,4},{6,5},{7,6},{8,7},{9,8},{10,9},{11,1... | collective-permute-start | bytes 27656 | tf_op jit(solution)/shard_map/ppermute | solution.py:21
  21.2 18.8 %reshape.93 = f32[8,2,16,2,64,2]{5,4,3,2,1,0:T(8,128)} reshape(f32[16,32,128]{2,1,0:T(8,128)} %param.3) | data formatting | bytes 524288 | tf_op jit(solution)/shard_map/reshape | solution.py:61
  40.0 7.0 reduce_sum.231
  56.8 5.7 collective-permute-start.6
  81.9 6.0 collective-permute-start.14
  89.9 6.0 collective-permute-start.10
  105.4 18.1 %reshape.92 = f32[8,2,16,2,64,2]{5,4,3,2,1,0:T(8,128)} reshape(f32[16,32,128]{2,1,0:T(8,128)S(1)} %fusion.22) | data formatting | bytes 524288 | tf_op jit(solution)/shard_map/reshape | solution.py:61
  123.5 7.0 reduce_sum.230
  161.6 6.0 collective-permute-start.22
  210.8 6.0 collective-permute-start.34
  239.1 79.6 %all_gather.7 = f32[2,256,16]{2,0,1:T(2,128)S(1)} all-gather(f32[2,4,16]{2,0,1:T(2,128)S(1)} %copy.324), channel_id=1, replica_groups=mesh['gx'=8,'yz'=64] {'yz'}, dimensions={1}, use_global_device_ids=true | all-gather | bytes 33280 | tf_op jit(solution)/shard_map/all_gather | solution.py:133
  338.1 80.3 %all_gather.6 = f32[2,256,16]{2,0,1:T(2,128)S(1)} all-gather(f32[2,4,16]{2,0,1:T(2,128)S(1)} %copy.321), channel_id=1, replica_groups=mesh['gx'=8,'yz'=64] {'yz'}, dimensions={1}, use_global_device_ids=true | all-gather | bytes 33280 | tf_op jit(solution)/shard_map/all_gather | solution.py:132
  428.3 11.3 %all-reduce.29 = (f32[]{:T(128)}, f32[]{:T(128)}) all-reduce(f32[]{:T(128)} %get-tuple-element.115, f32[]{:T(128)} %get-tuple-element.36), channel_id=1, replica_groups=mesh['gx'=8,'yz'=64] {'gx'}, use_global_device_ids=true, to_apply=%region_9.10 | all-reduce | flops 2 | bytes 16 | tf_op jit(solution)/shard_map/psum | solution.py:89
  450.4 11.0 %all-reduce.28 = (f32[]{:T(128)}, f32[]{:T(128)}) all-reduce(f32[]{:T(128)} %get-tuple-element.12, f32[]{:T(128)} %get-tuple-element.11), channel_id=1, replica_groups=mesh['gx'=8,'yz'=64] {'gx'}, use_global_device_ids=true, to_apply=%region_15.16 | all-reduce | flops 2 | bytes 16 | tf_op jit(solution)/shard_map/psum | solution.py:103
  465.8 11.9 %psum.116 = f32[]{:T(128)} all-reduce(f32[]{:T(128)} %multiply_reduce_fusion.11), channel_id=1, replica_groups=mesh['gx'=8,'yz'=64] {'gx'}, use_global_device_ids=true, to_apply=%region_19.20 | all-reduce | flops 1 | bytes 8 | tf_op jit(solution)/shard_map/psum | solution.py:109
  489.4 10.7 %psum.117 = f32[]{:T(128)} all-reduce(f32[]{:T(128)} %get-tuple-element.33), channel_id=1, replica_groups=mesh['gx'=8,'yz'=64] {'gx'}, use_global_device_ids=true, to_apply=%region_21.22 | all-reduce | flops 1 | bytes 8 | tf_op jit(solution)/shard_map/psum | solution.py:100
  509.7 11.0 %all-reduce.27 = (f32[]{:T(128)}, f32[]{:T(128)}) all-reduce(f32[]{:T(128)} %get-tuple-element.10, f32[]{:T(128)} %get-tuple-element.9), channel_id=1, replica_groups=mesh['gx'=8,'yz'=64] {'gx'}, use_global_device_ids=true, to_apply=%region_23.24 | all-reduce | flops 2 | bytes 16 | tf_op jit(solution)/shard_map/psum | solution.py:103
  525.1 12.1 %psum.120 = f32[]{:T(128)} all-reduce(f32[]{:T(128)} %get-tuple-element.30), channel_id=1, replica_groups=mesh['gx'=8,'yz'=64] {'gx'}, use_global_device_ids=true, to_apply=%region_27.28 | all-reduce | flops 1 | bytes 8 | tf_op jit(solution)/shard_map/psum | solution.py:109
  548.9 10.7 %psum.121 = f32[]{:T(128)} all-reduce(f32[]{:T(128)} %get-tuple-element.28), channel_id=1, replica_groups=mesh['gx'=8,'yz'=64] {'gx'}, use_global_device_ids=true, to_apply=%region_29.30 | all-reduce | flops 1 | bytes 8 | tf_op jit(solution)/shard_map/psum | solution.py:100
  569.3 11.0 %all-reduce.26 = (f32[]{:T(128)}, f32[]{:T(128)}) all-reduce(f32[]{:T(128)} %get-tuple-element.8, f32[]{:T(128)} %get-tuple-element.7), channel_id=1, replica_groups=mesh['gx'=8,'yz'=64] {'gx'}, use_global_device_ids=true, to_apply=%region_31.32 | all-reduce | flops 2 | bytes 16 | tf_op jit(solution)/shard_map/psum | solution.py:103
  584.7 12.1 %psum.124 = f32[]{:T(128)} all-reduce(f32[]{:T(128)} %get-tuple-element.25), channel_id=1, replica_groups=mesh['gx'=8,'yz'=64] {'gx'}, use_global_device_ids=true, to_apply=%region_35.36 | all-reduce | flops 1 | bytes 8 | tf_op jit(solution)/shard_map/psum | solution.py:109
  608.7 10.7 %psum.125 = f32[]{:T(128)} all-reduce(f32[]{:T(128)} %get-tuple-element.23), channel_id=1, replica_groups=mesh['gx'=8,'yz'=64] {'gx'}, use_global_device_ids=true, to_apply=%region_37.38 | all-reduce | flops 1 | bytes 8 | tf_op jit(solution)/shard_map/psum | solution.py:100
  629.1 11.0 %all-reduce.25 = (f32[]{:T(128)}, f32[]{:T(128)}) all-reduce(f32[]{:T(128)} %get-tuple-element.6, f32[]{:T(128)} %get-tuple-element.5), channel_id=1, replica_groups=mesh['gx'=8,'yz'=64] {'gx'}, use_global_device_ids=true, to_apply=%region_39.40 | all-reduce | flops 2 | bytes 16 | tf_op jit(solution)/shard_map/psum | solution.py:103
  656.6 5.6 collective-permute-done.69
  (346 shorter events, 315.2 us)
Async XLA Ops:
  7.7 39.3 %collective-permute-start.2 = (f32[18,1,128]{2,1,0:T(1,128)S(1)}, f32[18,1,128]{2,1,0:T(1,128)S(1)}, u32[]{:S(2)}, u32[]{:S(2)}) collective-permute-start(f32[18,1,128]{2,1,0:T(1,128)S(1)} %get-tuple-element.64), channel_id=1, source_target_pairs={{1,0},{2,1},{3,2},{4,3},{5,4},{6,5},{7,6},{8,7},{9,8},{10,9},{11,1... | collective-permute-start | bytes 27656 | tf_op jit(solution)/shard_map/ppermute | solution.py:21
  19.2 27.9 %collective-permute-start.3 = (f32[18,1,128]{2,1,0:T(1,128)S(1)}, f32[18,1,128]{2,1,0:T(1,128)S(1)}, u32[]{:S(2)}, u32[]{:S(2)}) collective-permute-start(f32[18,1,128]{2,1,0:T(1,128)S(1)} %get-tuple-element.63), channel_id=1, source_target_pairs={{0,1},{1,2},{2,3},{3,4},{4,5},{5,6},{6,7},{7,8},{8,9},{9,10},{10,1... | collective-permute-start | bytes 27656 | tf_op jit(solution)/shard_map/ppermute | solution.py:19
  56.8 15.6 %collective-permute-start.6 = (f32[18,1,128]{2,1,0:T(1,128)}, f32[18,1,128]{2,1,0:T(1,128)}, u32[]{:S(2)}, u32[]{:S(2)}) collective-permute-start(f32[18,1,128]{2,1,0:T(1,128)} %get-tuple-element.62), channel_id=1, source_target_pairs={{1,0},{2,1},{3,2},{4,3},{5,4},{6,5},{7,6},{8,7},{9,8},{10,9},{11,1... | collective-permute-start | bytes 27656 | tf_op jit(solution)/shard_map/ppermute | solution.py:21
  65.1 16.0 %collective-permute-start.12 = (f32[1,16,64]{2,1,0:T(8,128)}, f32[1,16,64]{2,1,0:T(8,128)}, u32[]{:S(2)}, u32[]{:S(2)}) collective-permute-start(f32[1,16,64]{2,1,0:T(8,128)} %get-tuple-element.88), channel_id=1, source_target_pairs={{64,0},{128,64},{192,128},{256,192},{320,256},{384,320},{448,384},... | collective-permute-start | bytes 12296 | tf_op jit(solution)/shard_map/ppermute | solution.py:21
  67.0 14.1 %collective-permute-start.13 = (f32[1,16,64]{2,1,0:T(8,128)}, f32[1,16,64]{2,1,0:T(8,128)}, u32[]{:S(2)}, u32[]{:S(2)}) collective-permute-start(f32[1,16,64]{2,1,0:T(8,128)} %get-tuple-element.87), channel_id=1, source_target_pairs={{0,64},{64,128},{128,192},{192,256},{256,320},{320,384},{384,448},... | collective-permute-start | bytes 12296 | tf_op jit(solution)/shard_map/ppermute | solution.py:19
  76.0 13.8 %collective-permute-start.8 = (f32[1,32,128]{2,1,0:T(8,128)S(1)}, f32[1,32,128]{2,1,0:T(8,128)S(1)}, u32[]{:S(2)}, u32[]{:S(2)}) collective-permute-start(f32[1,32,128]{2,1,0:T(8,128)S(1)} %get-tuple-element.68), channel_id=1, source_target_pairs={{64,0},{128,64},{192,128},{256,192},{320,256},{384,320},{448,384},... | collective-permute-start | bytes 49160 | tf_op jit(solution)/shard_map/ppermute | solution.py:21
  79.2 10.6 %collective-permute-start.9 = (f32[1,32,128]{2,1,0:T(8,128)S(1)}, f32[1,32,128]{2,1,0:T(8,128)S(1)}, u32[]{:S(2)}, u32[]{:S(2)}) collective-permute-start(f32[1,32,128]{2,1,0:T(8,128)S(1)} %get-tuple-element.67), channel_id=1, source_target_pairs={{0,64},{64,128},{128,192},{192,256},{256,320},{320,384},{384,448},... | collective-permute-start | bytes 49160 | tf_op jit(solution)/shard_map/ppermute | solution.py:19
  81.9 16.0 %collective-permute-start.14 = (f32[10,1,64]{2,1,0:T(1,128)S(1)}, f32[10,1,64]{2,1,0:T(1,128)S(1)}, u32[]{:S(2)}, u32[]{:S(2)}) collective-permute-start(f32[10,1,64]{2,1,0:T(1,128)S(1)} %get-tuple-element.80), channel_id=1, source_target_pairs={{1,0},{2,1},{3,2},{4,3},{5,4},{6,5},{7,6},{8,7},{9,8},{10,9},{11,1... | collective-permute-start | bytes 7688 | tf_op jit(solution)/shard_map/ppermute | solution.py:21
  87.9 10.0 %collective-permute-start.15 = (f32[10,1,64]{2,1,0:T(1,128)S(1)}, f32[10,1,64]{2,1,0:T(1,128)S(1)}, u32[]{:S(2)}, u32[]{:S(2)}) collective-permute-start(f32[10,1,64]{2,1,0:T(1,128)S(1)} %get-tuple-element.79), channel_id=1, source_target_pairs={{0,1},{1,2},{2,3},{3,4},{4,5},{5,6},{6,7},{7,8},{8,9},{9,10},{10,1... | collective-permute-start | bytes 7688 | tf_op jit(solution)/shard_map/ppermute | solution.py:19
  138.3 11.1 %collective-permute-start.18 = (f32[10,1,64]{2,1,0:T(1,128)S(1)}, f32[10,1,64]{2,1,0:T(1,128)S(1)}, u32[]{:S(2)}, u32[]{:S(2)}) collective-permute-start(f32[10,1,64]{2,1,0:T(1,128)S(1)} %get-tuple-element.78), channel_id=1, source_target_pairs={{1,0},{2,1},{3,2},{4,3},{5,4},{6,5},{7,6},{8,7},{9,8},{10,9},{11,1... | collective-permute-start | bytes 7688 | tf_op jit(solution)/shard_map/ppermute | solution.py:21
  144.2 11.3 %collective-permute-start.24 = (f32[1,8,32]{2,1,0:T(8,128)S(1)}, f32[1,8,32]{2,1,0:T(8,128)S(1)}, u32[]{:S(2)}, u32[]{:S(2)}) collective-permute-start(f32[1,8,32]{2,1,0:T(8,128)S(1)} %get-tuple-element.104), channel_id=1, source_target_pairs={{64,0},{128,64},{192,128},{256,192},{320,256},{384,320},{448,384},... | collective-permute-start | bytes 3080 | tf_op jit(solution)/shard_map/ppermute | solution.py:21
  150.4 11.1 %collective-permute-start.20 = (f32[1,16,64]{2,1,0:T(8,128)S(1)}, f32[1,16,64]{2,1,0:T(8,128)S(1)}, u32[]{:S(2)}, u32[]{:S(2)}) collective-permute-start(f32[1,16,64]{2,1,0:T(8,128)S(1)} %get-tuple-element.84), channel_id=1, source_target_pairs={{64,0},{128,64},{192,128},{256,192},{320,256},{384,320},{448,384},... | collective-permute-start | bytes 12296 | tf_op jit(solution)/shard_map/ppermute | solution.py:21
  155.6 14.2 %collective-permute-start.26 = (f32[6,1,32]{2,1,0:T(1,128)S(1)}, f32[6,1,32]{2,1,0:T(1,128)S(1)}, u32[]{:S(2)}, u32[]{:S(2)}) collective-permute-start(f32[6,1,32]{2,1,0:T(1,128)S(1)} %get-tuple-element.96), channel_id=1, source_target_pairs={{1,0},{2,1},{3,2},{4,3},{5,4},{6,5},{7,6},{8,7},{9,8},{10,9},{11,1... | collective-permute-start | bytes 2312 | tf_op jit(solution)/shard_map/ppermute | solution.py:21
  159.6 10.1 %collective-permute-start.27 = (f32[6,1,32]{2,1,0:T(1,128)S(1)}, f32[6,1,32]{2,1,0:T(1,128)S(1)}, u32[]{:S(2)}, u32[]{:S(2)}) collective-permute-start(f32[6,1,32]{2,1,0:T(1,128)S(1)} %get-tuple-element.95), channel_id=1, source_target_pairs={{0,1},{1,2},{2,3},{3,4},{4,5},{5,6},{6,7},{7,8},{8,9},{9,10},{10,1... | collective-permute-start | bytes 2312 | tf_op jit(solution)/shard_map/ppermute | solution.py:19
  188.6 10.2 %collective-permute-start.30 = (f32[6,1,32]{2,1,0:T(1,128)S(1)}, f32[6,1,32]{2,1,0:T(1,128)S(1)}, u32[]{:S(2)}, u32[]{:S(2)}) collective-permute-start(f32[6,1,32]{2,1,0:T(1,128)S(1)} %get-tuple-element.94), channel_id=1, source_target_pairs={{1,0},{2,1},{3,2},{4,3},{5,4},{6,5},{7,6},{8,7},{9,8},{10,9},{11,1... | collective-permute-start | bytes 2312 | tf_op jit(solution)/shard_map/ppermute | solution.py:21
  194.4 10.4 %collective-permute-start.36 = (f32[1,4,16]{2,1,0:T(4,128)S(1)}, f32[1,4,16]{2,1,0:T(4,128)S(1)}, u32[]{:S(2)}, u32[]{:S(2)}) collective-permute-start(f32[1,4,16]{2,1,0:T(4,128)S(1)} %get-tuple-element.122), channel_id=1, source_target_pairs={{64,0},{128,64},{192,128},{256,192},{320,256},{384,320},{448,384},... | collective-permute-start | bytes 776 | tf_op jit(solution)/shard_map/ppermute | solution.py:21
  199.7 11.1 %collective-permute-start.32 = (f32[1,8,32]{2,1,0:T(8,128)S(1)}, f32[1,8,32]{2,1,0:T(8,128)S(1)}, u32[]{:S(2)}, u32[]{:S(2)}) collective-permute-start(f32[1,8,32]{2,1,0:T(8,128)S(1)} %get-tuple-element.100), channel_id=1, source_target_pairs={{64,0},{128,64},{192,128},{256,192},{320,256},{384,320},{448,384},... | collective-permute-start | bytes 3080 | tf_op jit(solution)/shard_map/ppermute | solution.py:21
  204.8 14.0 %collective-permute-start.38 = (f32[4,1,16]{2,1,0:T(1,128)S(1)}, f32[4,1,16]{2,1,0:T(1,128)S(1)}, u32[]{:S(2)}, u32[]{:S(2)}) collective-permute-start(f32[4,1,16]{2,1,0:T(1,128)S(1)} %get-tuple-element.112), channel_id=1, source_target_pairs={{1,0},{2,1},{3,2},{4,3},{5,4},{6,5},{7,6},{8,7},{9,8},{10,9},{11,1... | collective-permute-start | bytes 776 | tf_op jit(solution)/shard_map/ppermute | solution.py:21
  208.9 9.9 %collective-permute-start.39 = (f32[4,1,16]{2,1,0:T(1,128)S(1)}, f32[4,1,16]{2,1,0:T(1,128)S(1)}, u32[]{:S(2)}, u32[]{:S(2)}) collective-permute-start(f32[4,1,16]{2,1,0:T(1,128)S(1)} %get-tuple-element.111), channel_id=1, source_target_pairs={{0,1},{1,2},{2,3},{3,4},{4,5},{5,6},{6,7},{7,8},{8,9},{9,10},{10,1... | collective-permute-start | bytes 776 | tf_op jit(solution)/shard_map/ppermute | solution.py:19
  233.3 85.4 %collective-permute-start.42 = (f32[4,1,16]{2,1,0:T(1,128)S(1)}, f32[4,1,16]{2,1,0:T(1,128)S(1)}, u32[]{:S(2)}, u32[]{:S(2)}) collective-permute-start(f32[4,1,16]{2,1,0:T(1,128)S(1)} %get-tuple-element.110), channel_id=1, source_target_pairs={{1,0},{2,1},{3,2},{4,3},{5,4},{6,5},{7,6},{8,7},{9,8},{10,9},{11,1... | collective-permute-start | bytes 776 | tf_op jit(solution)/shard_map/ppermute | solution.py:21
  235.2 83.5 %collective-permute-start.43 = (f32[4,1,16]{2,1,0:T(1,128)S(1)}, f32[4,1,16]{2,1,0:T(1,128)S(1)}, u32[]{:S(2)}, u32[]{:S(2)}) collective-permute-start(f32[4,1,16]{2,1,0:T(1,128)S(1)} %get-tuple-element.109), channel_id=1, source_target_pairs={{0,1},{1,2},{2,3},{3,4},{4,5},{5,6},{6,7},{7,8},{8,9},{9,10},{10,1... | collective-permute-start | bytes 776 | tf_op jit(solution)/shard_map/ppermute | solution.py:19
  325.7 10.9 %collective-permute-start.46 = (f32[4,1,16]{2,1,0:T(1,128)S(1)}, f32[4,1,16]{2,1,0:T(1,128)S(1)}, u32[]{:S(2)}, u32[]{:S(2)}) collective-permute-start(f32[4,1,16]{2,1,0:T(1,128)S(1)} %get-tuple-element.108), channel_id=1, source_target_pairs={{1,0},{2,1},{3,2},{4,3},{5,4},{6,5},{7,6},{8,7},{9,8},{10,9},{11,1... | collective-permute-start | bytes 776 | tf_op jit(solution)/shard_map/ppermute | solution.py:21
  332.3 92.7 %collective-permute-start.48 = (f32[1,128,8]{1,2,0:T(8,128)S(1)}, f32[1,128,8]{1,2,0:T(8,128)S(1)}, u32[]{:S(2)}, u32[]{:S(2)}) collective-permute-start(f32[1,128,8]{1,2,0:T(8,128)S(1)} %multiply_bitcast_fusion), channel_id=1, source_target_pairs={{64,0},{128,64},{192,128},{256,192},{320,256},{384,320},{448,384},... | collective-permute-start | bytes 12296 | tf_op jit(solution)/shard_map/ppermute | solution.py:21
  334.3 90.7 %collective-permute-start.50 = (f32[1,128,8]{1,2,0:T(8,128)S(1)}, f32[1,128,8]{1,2,0:T(8,128)S(1)}, u32[]{:S(2)}, u32[]{:S(2)}) collective-permute-start(f32[1,128,8]{1,2,0:T(8,128)S(1)} %multiply_bitcast_fusion), channel_id=1, source_target_pairs={{0,64},{64,128},{128,192},{192,256},{256,320},{320,384},{384,448},... | collective-permute-start | bytes 12296 | tf_op jit(solution)/shard_map/ppermute | solution.py:19
  (79 other events, 2040.2 us)
where the time goes:
time: 724 us; the launch traced here: 720 us
  blocking collectives  283 us (39%)
  starting transfers between devices  236 us (33%)
  waiting for transfers between devices  78.5 us (11%)
  local copies, waits for them, and re-layouts  50.6 us (7%)
  other arithmetic  48.4 us (7%)
  between operations  23.8 us (3%)
    ppermute x41, starting transfers between devices, padded_2(): lax.ppermute(head, axis, [((i + 1) % count, i) for i in range(ends)])  139 us
    ppermute x41, starting transfers between devices, padded_2(): lax.ppermute(tail, axis, [(i, (i + 1) % count) for i in range(ends)])  96.7 us
    all_gather x1, blocking collectives, per_device(): lax.all_gather(residual, 'yz', axis=1, tiled=True)  80.3 us
    all_gather x1, blocking collectives, per_device(): lax.all_gather(weight, 'yz', axis=1, tiled=True)  79.6 us
    ppermute x41, waiting for transfers between devices, padded_2(): lax.ppermute(tail, axis, [(i, (i + 1) % count) for i in range(ends)])  78 us
    psum x4, blocking collectives, stabilized_solve(): rho_now = lax.psum(jnp.sum(source * residual), 'gx')  47.4 us
    psum x4, blocking collectives, stabilized_solve(): lax.psum((jnp.sum(bent_image * middle), jnp.sum(bent_image * bent_image))...  43.9 us
    reshape x4, local copies, waits for them, and re-layouts, restrict(): values.reshape(values.shape[0] // 2, 2, values.shape[1] // 2, 2, values.s...  40 us
  transfers between devices with their start and end apart: 82, of which 26 were waited for; matrix products, arithmetic and copies ran while one was open for 6% of the time, Pallas kernels for 0%

commit v1 on v0

--- a/solution.py
+++ b/solution.py
@@ -6,6 +6,18 @@
 LEVELS = 4
 BITERS = 4
 RELAXATION = 0.8
+
+
+def doubled_up(x, axis, dim):
+    ways, here = (lax.axis_size(axis), lax.axis_index(axis))
+    grown, reach = (x, 1)
+    while reach < ways:
+        theirs = lax.ppermute(grown, axis, [(d, d ^ reach) for d in range(ways)])
+        mine_first = jnp.concatenate([grown, theirs], axis=dim)
+        theirs_first = jnp.concatenate([theirs, grown], axis=dim)
+        grown = jnp.where(here & reach == 0, mine_first, theirs_first)
+        reach = 2 * reach
+    return grown
 
 
 def padded_2(cells, sides, width):
@@ -129,7 +141,7 @@
         stored.append((source, iterate, face_list, diagonal, merged))
         if level_index == LEVELS - 1:
             residual, weight = (
-                lax.all_gather(residual, "yz", axis=1, tiled=True),
+                doubled_up(residual, "yz", 1),
                 lax.all_gather(weight, "yz", axis=1, tiled=True),
             )
         source = restrict(residual)

time: 724 us -> 692 us (0.956)
  blocking collectives: 283 us -> 203 us
  waiting for transfers between devices: 78.5 us -> 115 us
  starting transfers between devices: 236 us -> 249 us
    all_gather x1 -> x0, blocking collectives: 80.3 us -> none  [per_device(): lax.all_gather(residual, 'yz', axis=1, tiled=True)]
    ppermute x0 -> x6, waiting for transfers between devices: none -> 28.2 us  [doubled_up(): theirs = lax.ppermute(grown, axis, [(d, d ^ reach) for d in range(ways)])]
    ppermute x0 -> x6, starting transfers between devices: none -> 13.5 us  [doubled_up(): theirs = lax.ppermute(grown, axis, [(d, d ^ reach) for d in range(ways)])]
    ppermute x41, waiting for transfers between devices: 78 us -> 85.9 us  [padded_2(): lax.ppermute(tail, axis, [(i, (i + 1) % count) for i in range(ends)])]
  transfers between devices with their start and end apart: 82 -> 88, of which waited for: 26 -> 31; matrix products, arithmetic and copies ran while one was open for 6% -> 6% of each run, Pallas kernels for 0% -> 0%
where the time goes in v1:
time: 692 us; the launch traced here: 688 us
  starting transfers between devices  249 us (36%)
  blocking collectives  203 us (29%)
  waiting for transfers between devices  115 us (17%)
  local copies, waits for them, and re-layouts  48.8 us (7%)
  other arithmetic  48.6 us (7%)
  between operations  23.8 us (3%)
    ppermute x41, starting transfers between devices, padded_2(): lax.ppermute(head, axis, [((i + 1) % count, i) for i in range(ends)])  137 us
    ppermute x41, starting transfers between devices, padded_2(): lax.ppermute(tail, axis, [(i, (i + 1) % count) for i in range(ends)])  98.6 us
    ppermute x41, waiting for transfers between devices, padded_2(): lax.ppermute(tail, axis, [(i, (i + 1) % count) for i in range(ends)])  85.9 us
    all_gather x1, blocking collectives, per_device(): lax.all_gather(weight, 'yz', axis=1, tiled=True)  81 us
    psum x4, blocking collectives, stabilized_solve(): rho_now = lax.psum(jnp.sum(source * residual), 'gx')  46.4 us
    psum x4, blocking collectives, stabilized_solve(): lax.psum((jnp.sum(bent_image * middle), jnp.sum(bent_image * bent_image))...  43.9 us
    reshape x4, local copies, waits for them, and re-layouts, restrict(): values.reshape(values.shape[0] // 2, 2, values.shape[1] // 2, 2, values.s...  40 us
    psum x3, blocking collectives, stabilized_solve(): step_alpha = rho_now / lax.psum(jnp.sum(source * applied), 'gx')  31.9 us
  transfers between devices with their start and end apart: 88, of which 31 were waited for; matrix products, arithmetic and copies ran while one was open for 6% of the time, Pallas kernels for 0%

profile of v1, /device:TPU:10, one launch (start us, length us, event | category | flops | bytes accessed | tf_op | source)
XLA Modules:
  0.0 688.3 jit_solution(15965558743324618509)
XLA Ops:
  7.7 11.4 %collective-permute-start.2 = (f32[18,1,128]{2,1,0:T(1,128)S(1)}, f32[18,1,128]{2,1,0:T(1,128)S(1)}, u32[]{:S(2)}, u32[]{:S(2)}) collective-permute-start(f32[18,1,128]{2,1,0:T(1,128)S(1)} %get-tuple-element.64), channel_id=1, source_target_pairs={{1,0},{2,1},{3,2},{4,3},{5,4},{6,5},{7,6},{8,7},{9,8},{10,9},{11,1... | collective-permute-start | bytes 27656 | tf_op jit(solution)/shard_map/ppermute | solution.py:33
  21.2 18.8 %reshape.95 = f32[8,2,16,2,64,2]{5,4,3,2,1,0:T(8,128)} reshape(f32[16,32,128]{2,1,0:T(8,128)} %param.3) | data formatting | bytes 524288 | tf_op jit(solution)/shard_map/reshape | solution.py:73
  40.0 7.0 %reduce_sum.231 = f32[8,16,64]{2,1,0:T(8,128)S(1)} reduce(f32[8,2,16,2,64,2]{5,4,3,2,1,0:T(8,128)} %reshape.95, f32[]{:T(128)} %constant.20.clone.1), dimensions={1,3,5}, to_apply=%region_1.2 | reduce | flops 57344 | bytes 294916 | tf_op jit(solution)/shard_map/reduce_sum | solution.py:75
  56.8 5.7 collective-permute-start.6
  81.9 6.0 collective-permute-start.14
  89.9 6.0 collective-permute-start.10
  105.5 18.1 %reshape.94 = f32[8,2,16,2,64,2]{5,4,3,2,1,0:T(8,128)} reshape(f32[16,32,128]{2,1,0:T(8,128)S(1)} %fusion.22) | data formatting | bytes 524288 | tf_op jit(solution)/shard_map/reshape | solution.py:73
  123.5 7.0 %reduce_sum.230 = f32[8,16,64]{2,1,0:T(8,128)S(1)} reduce(f32[8,2,16,2,64,2]{5,4,3,2,1,0:T(8,128)} %reshape.94, f32[]{:T(128)} %constant.20.clone.1), dimensions={1,3,5}, to_apply=%region_0.1 | reduce | flops 57344 | bytes 294916 | tf_op jit(solution)/shard_map/reduce_sum | solution.py:75
  161.6 6.0 collective-permute-start.22
  210.9 6.0 collective-permute-start.34
  273.4 7.6 %collective-permute-done.50 = f32[2,16,16]{2,1,0:T(8,128)S(1)} collective-permute-done((f32[2,16,16]{2,1,0:T(8,128)S(1)}, f32[2,16,16]{2,1,0:T(8,128)S(1)}, u32[]{:S(2)}, u32[]{:S(2)}) %collective-permute-start.50) | collective-permute-done | bytes 2080 | tf_op jit(solution)/shard_map/ppermute | solution.py:15
  283.0 12.5 %collective-permute-done.51 = f32[2,32,16]{2,1,0:T(8,128)S(1)} collective-permute-done((f32[2,32,16]{2,1,0:T(8,128)S(1)}, f32[2,32,16]{2,1,0:T(8,128)S(1)}, u32[]{:S(2)}, u32[]{:S(2)}) %collective-permute-start.51) | collective-permute-done | bytes 4128 | tf_op jit(solution)/shard_map/ppermute | solution.py:15
  297.6 81.0 %all_gather.3 = f32[2,256,16]{2,0,1:T(2,128)S(1)} all-gather(f32[2,4,16]{2,0,1:T(2,128)S(1)} %copy.337), channel_id=1, replica_groups=mesh['gx'=8,'yz'=64] {'yz'}, dimensions={1}, use_global_device_ids=true | all-gather | bytes 33280 | tf_op jit(solution)/shard_map/all_gather | solution.py:145
  399.5 10.7 %all-reduce.29 = (f32[]{:T(128)}, f32[]{:T(128)}) all-reduce(f32[]{:T(128)} %get-tuple-element.115, f32[]{:T(128)} %get-tuple-element.36), channel_id=1, replica_groups=mesh['gx'=8,'yz'=64] {'gx'}, use_global_device_ids=true, to_apply=%region_9.10 | all-reduce | flops 2 | bytes 16 | tf_op jit(solution)/shard_map/psum | solution.py:101
  421.5 11.0 %all-reduce.28 = (f32[]{:T(128)}, f32[]{:T(128)}) all-reduce(f32[]{:T(128)} %get-tuple-element.12, f32[]{:T(128)} %get-tuple-element.11), channel_id=1, replica_groups=mesh['gx'=8,'yz'=64] {'gx'}, use_global_device_ids=true, to_apply=%region_15.16 | all-reduce | flops 2 | bytes 16 | tf_op jit(solution)/shard_map/psum | solution.py:115
  436.9 11.6 %psum.116 = f32[]{:T(128)} all-reduce(f32[]{:T(128)} %multiply_reduce_fusion.11), channel_id=1, replica_groups=mesh['gx'=8,'yz'=64] {'gx'}, use_global_device_ids=true, to_apply=%region_19.20 | all-reduce | flops 1 | bytes 8 | tf_op jit(solution)/shard_map/psum | solution.py:121
  460.5 10.6 %psum.117 = f32[]{:T(128)} all-reduce(f32[]{:T(128)} %get-tuple-element.33), channel_id=1, replica_groups=mesh['gx'=8,'yz'=64] {'gx'}, use_global_device_ids=true, to_apply=%region_21.22 | all-reduce | flops 1 | bytes 8 | tf_op jit(solution)/shard_map/psum | solution.py:112
  480.9 10.9 %all-reduce.27 = (f32[]{:T(128)}, f32[]{:T(128)}) all-reduce(f32[]{:T(128)} %get-tuple-element.10, f32[]{:T(128)} %get-tuple-element.9), channel_id=1, replica_groups=mesh['gx'=8,'yz'=64] {'gx'}, use_global_device_ids=true, to_apply=%region_23.24 | all-reduce | flops 2 | bytes 16 | tf_op jit(solution)/shard_map/psum | solution.py:115
  496.2 12.1 %psum.120 = f32[]{:T(128)} all-reduce(f32[]{:T(128)} %get-tuple-element.30), channel_id=1, replica_groups=mesh['gx'=8,'yz'=64] {'gx'}, use_global_device_ids=true, to_apply=%region_27.28 | all-reduce | flops 1 | bytes 8 | tf_op jit(solution)/shard_map/psum | solution.py:121
  520.1 10.6 %psum.121 = f32[]{:T(128)} all-reduce(f32[]{:T(128)} %get-tuple-element.28), channel_id=1, replica_groups=mesh['gx'=8,'yz'=64] {'gx'}, use_global_device_ids=true, to_apply=%region_29.30 | all-reduce | flops 1 | bytes 8 | tf_op jit(solution)/shard_map/psum | solution.py:112
  540.4 11.0 %all-reduce.26 = (f32[]{:T(128)}, f32[]{:T(128)}) all-reduce(f32[]{:T(128)} %get-tuple-element.8, f32[]{:T(128)} %get-tuple-element.7), channel_id=1, replica_groups=mesh['gx'=8,'yz'=64] {'gx'}, use_global_device_ids=true, to_apply=%region_31.32 | all-reduce | flops 2 | bytes 16 | tf_op jit(solution)/shard_map/psum | solution.py:115
  555.8 12.0 %psum.124 = f32[]{:T(128)} all-reduce(f32[]{:T(128)} %get-tuple-element.25), channel_id=1, replica_groups=mesh['gx'=8,'yz'=64] {'gx'}, use_global_device_ids=true, to_apply=%region_35.36 | all-reduce | flops 1 | bytes 8 | tf_op jit(solution)/shard_map/psum | solution.py:121
  579.5 10.6 %psum.125 = f32[]{:T(128)} all-reduce(f32[]{:T(128)} %get-tuple-element.23), channel_id=1, replica_groups=mesh['gx'=8,'yz'=64] {'gx'}, use_global_device_ids=true, to_apply=%region_37.38 | all-reduce | flops 1 | bytes 8 | tf_op jit(solution)/shard_map/psum | solution.py:112
  599.7 11.0 %all-reduce.25 = (f32[]{:T(128)}, f32[]{:T(128)}) all-reduce(f32[]{:T(128)} %get-tuple-element.6, f32[]{:T(128)} %get-tuple-element.5), channel_id=1, replica_groups=mesh['gx'=8,'yz'=64] {'gx'}, use_global_device_ids=true, to_apply=%region_39.40 | all-reduce | flops 2 | bytes 16 | tf_op jit(solution)/shard_map/psum | solution.py:115
  (366 shorter events, 349.0 us)
Async XLA Ops:
  7.7 39.3 %collective-permute-start.2 = (f32[18,1,128]{2,1,0:T(1,128)S(1)}, f32[18,1,128]{2,1,0:T(1,128)S(1)}, u32[]{:S(2)}, u32[]{:S(2)}) collective-permute-start(f32[18,1,128]{2,1,0:T(1,128)S(1)} %get-tuple-element.64), channel_id=1, source_target_pairs={{1,0},{2,1},{3,2},{4,3},{5,4},{6,5},{7,6},{8,7},{9,8},{10,9},{11,1... | collective-permute-start | bytes 27656 | tf_op jit(solution)/shard_map/ppermute | solution.py:33
  19.2 27.9 %collective-permute-start.3 = (f32[18,1,128]{2,1,0:T(1,128)S(1)}, f32[18,1,128]{2,1,0:T(1,128)S(1)}, u32[]{:S(2)}, u32[]{:S(2)}) collective-permute-start(f32[18,1,128]{2,1,0:T(1,128)S(1)} %get-tuple-element.63), channel_id=1, source_target_pairs={{0,1},{1,2},{2,3},{3,4},{4,5},{5,6},{6,7},{7,8},{8,9},{9,10},{10,1... | collective-permute-start | bytes 27656 | tf_op jit(solution)/shard_map/ppermute | solution.py:31
  56.8 15.6 %collective-permute-start.6 = (f32[18,1,128]{2,1,0:T(1,128)}, f32[18,1,128]{2,1,0:T(1,128)}, u32[]{:S(2)}, u32[]{:S(2)}) collective-permute-start(f32[18,1,128]{2,1,0:T(1,128)} %get-tuple-element.62), channel_id=1, source_target_pairs={{1,0},{2,1},{3,2},{4,3},{5,4},{6,5},{7,6},{8,7},{9,8},{10,9},{11,1... | collective-permute-start | bytes 27656 | tf_op jit(solution)/shard_map/ppermute | solution.py:33
  62.5 9.9 %collective-permute-start.7 = (f32[18,1,128]{2,1,0:T(1,128)}, f32[18,1,128]{2,1,0:T(1,128)}, u32[]{:S(2)}, u32[]{:S(2)}) collective-permute-start(f32[18,1,128]{2,1,0:T(1,128)} %get-tuple-element.61), channel_id=1, source_target_pairs={{0,1},{1,2},{2,3},{3,4},{4,5},{5,6},{6,7},{7,8},{8,9},{9,10},{10,1... | collective-permute-start | bytes 27656 | tf_op jit(solution)/shard_map/ppermute | solution.py:31
  65.1 16.1 %collective-permute-start.12 = (f32[1,16,64]{2,1,0:T(8,128)}, f32[1,16,64]{2,1,0:T(8,128)}, u32[]{:S(2)}, u32[]{:S(2)}) collective-permute-start(f32[1,16,64]{2,1,0:T(8,128)} %get-tuple-element.88), channel_id=1, source_target_pairs={{64,0},{128,64},{192,128},{256,192},{320,256},{384,320},{448,384},... | collective-permute-start | bytes 12296 | tf_op jit(solution)/shard_map/ppermute | solution.py:33
  67.0 14.2 %collective-permute-start.13 = (f32[1,16,64]{2,1,0:T(8,128)}, f32[1,16,64]{2,1,0:T(8,128)}, u32[]{:S(2)}, u32[]{:S(2)}) collective-permute-start(f32[1,16,64]{2,1,0:T(8,128)} %get-tuple-element.87), channel_id=1, source_target_pairs={{0,64},{64,128},{128,192},{192,256},{256,320},{320,384},{384,448},... | collective-permute-start | bytes 12296 | tf_op jit(solution)/shard_map/ppermute | solution.py:31
  76.1 13.8 %collective-permute-start.8 = (f32[1,32,128]{2,1,0:T(8,128)S(1)}, f32[1,32,128]{2,1,0:T(8,128)S(1)}, u32[]{:S(2)}, u32[]{:S(2)}) collective-permute-start(f32[1,32,128]{2,1,0:T(8,128)S(1)} %get-tuple-element.68), channel_id=1, source_target_pairs={{64,0},{128,64},{192,128},{256,192},{320,256},{384,320},{448,384},... | collective-permute-start | bytes 49160 | tf_op jit(solution)/shard_map/ppermute | solution.py:33
  79.2 10.6 %collective-permute-start.9 = (f32[1,32,128]{2,1,0:T(8,128)S(1)}, f32[1,32,128]{2,1,0:T(8,128)S(1)}, u32[]{:S(2)}, u32[]{:S(2)}) collective-permute-start(f32[1,32,128]{2,1,0:T(8,128)S(1)} %get-tuple-element.67), channel_id=1, source_target_pairs={{0,64},{64,128},{128,192},{192,256},{256,320},{320,384},{384,448},... | collective-permute-start | bytes 49160 | tf_op jit(solution)/shard_map/ppermute | solution.py:31
  81.9 16.0 %collective-permute-start.14 = (f32[10,1,64]{2,1,0:T(1,128)S(1)}, f32[10,1,64]{2,1,0:T(1,128)S(1)}, u32[]{:S(2)}, u32[]{:S(2)}) collective-permute-start(f32[10,1,64]{2,1,0:T(1,128)S(1)} %get-tuple-element.80), channel_id=1, source_target_pairs={{1,0},{2,1},{3,2},{4,3},{5,4},{6,5},{7,6},{8,7},{9,8},{10,9},{11,1... | collective-permute-start | bytes 7688 | tf_op jit(solution)/shard_map/ppermute | solution.py:33
  87.9 10.0 %collective-permute-start.15 = (f32[10,1,64]{2,1,0:T(1,128)S(1)}, f32[10,1,64]{2,1,0:T(1,128)S(1)}, u32[]{:S(2)}, u32[]{:S(2)}) collective-permute-start(f32[10,1,64]{2,1,0:T(1,128)S(1)} %get-tuple-element.79), channel_id=1, source_target_pairs={{0,1},{1,2},{2,3},{3,4},{4,5},{5,6},{6,7},{7,8},{8,9},{9,10},{10,1... | collective-permute-start | bytes 7688 | tf_op jit(solution)/shard_map/ppermute | solution.py:31
  138.4 11.1 %collective-permute-start.18 = (f32[10,1,64]{2,1,0:T(1,128)S(1)}, f32[10,1,64]{2,1,0:T(1,128)S(1)}, u32[]{:S(2)}, u32[]{:S(2)}) collective-permute-start(f32[10,1,64]{2,1,0:T(1,128)S(1)} %get-tuple-element.78), channel_id=1, source_target_pairs={{1,0},{2,1},{3,2},{4,3},{5,4},{6,5},{7,6},{8,7},{9,8},{10,9},{11,1... | collective-permute-start | bytes 7688 | tf_op jit(solution)/shard_map/ppermute | solution.py:33
  144.3 11.3 %collective-permute-start.24 = (f32[1,8,32]{2,1,0:T(8,128)S(1)}, f32[1,8,32]{2,1,0:T(8,128)S(1)}, u32[]{:S(2)}, u32[]{:S(2)}) collective-permute-start(f32[1,8,32]{2,1,0:T(8,128)S(1)} %get-tuple-element.104), channel_id=1, source_target_pairs={{64,0},{128,64},{192,128},{256,192},{320,256},{384,320},{448,384},... | collective-permute-start | bytes 3080 | tf_op jit(solution)/shard_map/ppermute | solution.py:33
  150.5 11.1 %collective-permute-start.20 = (f32[1,16,64]{2,1,0:T(8,128)S(1)}, f32[1,16,64]{2,1,0:T(8,128)S(1)}, u32[]{:S(2)}, u32[]{:S(2)}) collective-permute-start(f32[1,16,64]{2,1,0:T(8,128)S(1)} %get-tuple-element.84), channel_id=1, source_target_pairs={{64,0},{128,64},{192,128},{256,192},{320,256},{384,320},{448,384},... | collective-permute-start | bytes 12296 | tf_op jit(solution)/shard_map/ppermute | solution.py:33
  155.6 14.2 %collective-permute-start.26 = (f32[6,1,32]{2,1,0:T(1,128)S(1)}, f32[6,1,32]{2,1,0:T(1,128)S(1)}, u32[]{:S(2)}, u32[]{:S(2)}) collective-permute-start(f32[6,1,32]{2,1,0:T(1,128)S(1)} %get-tuple-element.96), channel_id=1, source_target_pairs={{1,0},{2,1},{3,2},{4,3},{5,4},{6,5},{7,6},{8,7},{9,8},{10,9},{11,1... | collective-permute-start | bytes 2312 | tf_op jit(solution)/shard_map/ppermute | solution.py:33
  159.7 10.1 %collective-permute-start.27 = (f32[6,1,32]{2,1,0:T(1,128)S(1)}, f32[6,1,32]{2,1,0:T(1,128)S(1)}, u32[]{:S(2)}, u32[]{:S(2)}) collective-permute-start(f32[6,1,32]{2,1,0:T(1,128)S(1)} %get-tuple-element.95), channel_id=1, source_target_pairs={{0,1},{1,2},{2,3},{3,4},{4,5},{5,6},{6,7},{7,8},{8,9},{9,10},{10,1... | collective-permute-start | bytes 2312 | tf_op jit(solution)/shard_map/ppermute | solution.py:31
  188.6 10.2 %collective-permute-start.30 = (f32[6,1,32]{2,1,0:T(1,128)S(1)}, f32[6,1,32]{2,1,0:T(1,128)S(1)}, u32[]{:S(2)}, u32[]{:S(2)}) collective-permute-start(f32[6,1,32]{2,1,0:T(1,128)S(1)} %get-tuple-element.94), channel_id=1, source_target_pairs={{1,0},{2,1},{3,2},{4,3},{5,4},{6,5},{7,6},{8,7},{9,8},{10,9},{11,1... | collective-permute-start | bytes 2312 | tf_op jit(solution)/shard_map/ppermute | solution.py:33
  194.5 10.4 %collective-permute-start.36 = (f32[1,4,16]{2,1,0:T(4,128)S(1)}, f32[1,4,16]{2,1,0:T(4,128)S(1)}, u32[]{:S(2)}, u32[]{:S(2)}) collective-permute-start(f32[1,4,16]{2,1,0:T(4,128)S(1)} %get-tuple-element.122), channel_id=1, source_target_pairs={{64,0},{128,64},{192,128},{256,192},{320,256},{384,320},{448,384},... | collective-permute-start | bytes 776 | tf_op jit(solution)/shard_map/ppermute | solution.py:33
  199.8 11.1 %collective-permute-start.32 = (f32[1,8,32]{2,1,0:T(8,128)S(1)}, f32[1,8,32]{2,1,0:T(8,128)S(1)}, u32[]{:S(2)}, u32[]{:S(2)}) collective-permute-start(f32[1,8,32]{2,1,0:T(8,128)S(1)} %get-tuple-element.100), channel_id=1, source_target_pairs={{64,0},{128,64},{192,128},{256,192},{320,256},{384,320},{448,384},... | collective-permute-start | bytes 3080 | tf_op jit(solution)/shard_map/ppermute | solution.py:33
  204.9 14.0 %collective-permute-start.38 = (f32[4,1,16]{2,1,0:T(1,128)S(1)}, f32[4,1,16]{2,1,0:T(1,128)S(1)}, u32[]{:S(2)}, u32[]{:S(2)}) collective-permute-start(f32[4,1,16]{2,1,0:T(1,128)S(1)} %get-tuple-element.112), channel_id=1, source_target_pairs={{1,0},{2,1},{3,2},{4,3},{5,4},{6,5},{7,6},{8,7},{9,8},{10,9},{11,1... | collective-permute-start | bytes 776 | tf_op jit(solution)/shard_map/ppermute | solution.py:33
  208.9 9.9 %collective-permute-start.39 = (f32[4,1,16]{2,1,0:T(1,128)S(1)}, f32[4,1,16]{2,1,0:T(1,128)S(1)}, u32[]{:S(2)}, u32[]{:S(2)}) collective-permute-start(f32[4,1,16]{2,1,0:T(1,128)S(1)} %get-tuple-element.111), channel_id=1, source_target_pairs={{0,1},{1,2},{2,3},{3,4},{4,5},{5,6},{6,7},{7,8},{8,9},{9,10},{10,1... | collective-permute-start | bytes 776 | tf_op jit(solution)/shard_map/ppermute | solution.py:31
  271.5 9.5 %collective-permute-start.50 = (f32[2,16,16]{2,1,0:T(8,128)S(1)}, f32[2,16,16]{2,1,0:T(8,128)S(1)}, u32[]{:S(2)}, u32[]{:S(2)}) collective-permute-start(f32[2,16,16]{2,1,0:T(8,128)S(1)} %maximum_select_fusion.2), channel_id=1, source_target_pairs={{0,4},{1,5},{2,6},{3,7},{4,0},{5,1},{6,2},{7,3},{8,12},{9,13},{10,... | collective-permute-start | bytes 6152 | tf_op jit(solution)/shard_map/ppermute | solution.py:15
  281.0 14.5 %collective-permute-start.51 = (f32[2,32,16]{2,1,0:T(8,128)S(1)}, f32[2,32,16]{2,1,0:T(8,128)S(1)}, u32[]{:S(2)}, u32[]{:S(2)}) collective-permute-start(f32[2,32,16]{2,1,0:T(8,128)S(1)} %maximum_select_fusion), channel_id=1, source_target_pairs={{0,8},{1,9},{2,10},{3,11},{4,12},{5,13},{6,14},{7,15},{8,0},{9,1},... | collective-permute-start | bytes 12296 | tf_op jit(solution)/shard_map/ppermute | solution.py:15
  295.7 84.6 %collective-permute-start.52 = (f32[2,64,16]{1,2,0:T(8,128)S(1)}, f32[2,64,16]{1,2,0:T(8,128)S(1)}, u32[]{:S(2)}, u32[]{:S(2)}) collective-permute-start(f32[2,64,16]{1,2,0:T(8,128)S(1)} %maximum_select_fusion.3), channel_id=1, source_target_pairs={{0,16},{1,17},{2,18},{3,19},{4,20},{5,21},{6,22},{7,23},{8,24},{9,... | collective-permute-start | bytes 24584 | tf_op jit(solution)/shard_map/ppermute | solution.py:15
  384.3 11.3 %collective-permute-start.54 = (f32[1,128,8]{1,2,0:T(8,128)S(1)}, f32[1,128,8]{1,2,0:T(8,128)S(1)}, u32[]{:S(2)}, u32[]{:S(2)}) collective-permute-start(f32[1,128,8]{1,2,0:T(8,128)S(1)} %multiply_bitcast_fusion), channel_id=1, source_target_pairs={{64,0},{128,64},{192,128},{256,192},{320,256},{384,320},{448,384},... | collective-permute-start | bytes 12296 | tf_op jit(solution)/shard_map/ppermute | solution.py:33
  (87 other events, 3019.1 us)
